TPU v7x, 256 devices: a whole 4x4x8 slice. The times are simulated.
256 devices in a mesh: tm: 16 (over x_lo, y, core), rows: 16 (over x_hi, z).
Axes of the slice: x: 4 (x_hi: 2, x_lo: 2; x = x_hi * 2 + x_lo), y: 4, z: 8, core: 2. Of those that a mesh axis runs over, the one named last changes fastest.
Arguments:
- latents: bfloat16 [48, 16, 16, 768], P('tm', 'rows'), may hold values from -105 to 105
- first_gain: float32 [768], replicated, may hold values from 0.1 to 1.9
- first_bias: float32 [768], replicated, may hold values from -3 to 3
- second_gain: float32 [768], replicated, may hold values from 0.1 to 1.9
- second_bias: float32 [768], replicated, may hold values from -3 to 3
- first_kernel: bfloat16 [3, 3, 3, 768, 768], P(None, None, None, 'rows'), may hold values from -0.0390625 to 0.0390625
- second_kernel: bfloat16 [3, 3, 3, 768, 768], P(None, None, None, 'rows'), may hold values from -0.0390625 to 0.0390625
- expand_kernel: bfloat16 [768, 6144], P(None, 'rows'), may hold values from -0.21875 to 0.21875
Outputs:
- decoded: bfloat16 [144, 32, 32, 512], P('tm', 'rows')
All inputs are finite; a program needn't handle non-finite values.
Results may differ from a plain program's by a relative error of at most 0.0051.
Values may be sent and summed in bfloat16 or wider, within the bound.
A program may use at most 128 MiB of HBM per device.

v0:
```python
import jax
import jax.numpy as jnp
from jax import lax
from jax.sharding import PartitionSpec as P

GROUPS = 32


def from_behind(block, axis, distance):
    devices = range(lax.axis_size(axis))
    route = [(i - distance, i) for i in devices if i - distance in devices]
    return lax.ppermute(block, axis, route)


def past_small(field):
    return from_behind(field, "tm", 1)


def gather_rows(field):
    return lax.all_gather(field, "rows", axis=1, tiled=True)


def gather_channels(field):
    return lax.all_gather(field, "rows", axis=3, tiled=True)


def channel_sums(field):
    values = field.astype(jnp.float32)
    return (jnp.sum(values, axis=(0, 1, 2)), jnp.sum(values * values, axis=(0, 1, 2)))


def stats_gathered(own_block):
    chan_sum, chan_square = channel_sums(own_block)
    return lax.psum((chan_sum, chan_square), "tm")


def prepare(whole, chan_sum, chan_square, total_count, gain, shift_bias, at_start):
    chan_total = whole.shape[3]
    per_group = chan_total // GROUPS
    group_sum = chan_sum.reshape(GROUPS, per_group).sum(1)
    group_square = chan_square.reshape(GROUPS, per_group).sum(1)
    average = group_sum / total_count
    spread = group_square / total_count - average * average
    inv_scale = lax.rsqrt(spread + 1e-06)
    chan_average = jnp.repeat(average, per_group)
    chan_scale = jnp.repeat(inv_scale, per_group)
    normed = (whole.astype(jnp.float32) - chan_average) * chan_scale * gain + shift_bias
    active = jax.nn.silu(normed).astype(jnp.bfloat16)
    keeping = jnp.logical_or(jnp.arange(active.shape[0]) >= 2, jnp.logical_not(at_start))
    active = jnp.where(keeping[:, None, None, None], active, jnp.zeros_like(active))
    return jnp.pad(active, ((0, 0), (1, 1), (1, 1), (0, 0)))


def local_conv(padded, kernel, frames_n):
    rows_n = padded.shape[1] - 2
    width_n = padded.shape[2] - 2
    total = jnp.zeros((frames_n, rows_n, width_n, kernel.shape[3]), jnp.float32)
    for tap_time in range(3):
        for tap_row in range(3):
            for tap_col in range(3):
                window = padded[
                    tap_time : tap_time + frames_n,
                    tap_row : tap_row + rows_n,
                    tap_col : tap_col + width_n,
                ]
                total = total + jnp.einsum(
                    "thwc,dc->thwd",
                    window,
                    kernel[tap_time, tap_row, tap_col],
                    preferred_element_type=jnp.float32,
                )
    return total


def depth_space(expanded):
    frames_n, rows_n, width_n = (expanded.shape[0], expanded.shape[1], expanded.shape[2])
    out_chan = expanded.shape[3] // 12
    parted = expanded.reshape(frames_n, rows_n, width_n, out_chan, 3, 2, 2)
    moved = parted.transpose(0, 4, 1, 5, 2, 6, 3)
    return moved.reshape(frames_n * 3, rows_n * 2, width_n * 2, out_chan)


def shards(
    latents,
    first_gain,
    first_bias,
    second_gain,
    second_bias,
    first_kernel,
    second_kernel,
    expand_kernel,
):
    frames_n = latents.shape[0]
    chan_total = latents.shape[3]
    chan_part = first_kernel.shape[3]
    at_start = lax.axis_index("tm") == 0
    offset = lax.axis_index("rows") * chan_part
    time_total = frames_n * lax.axis_size("tm")
    whole_x = gather_rows(jnp.concatenate([past_small(latents[-2:]), latents], 0))
    own_x = whole_x[2:]
    total_count = time_total * own_x.shape[1] * own_x.shape[2] * (chan_total // GROUPS)
    chan_sum, chan_square = stats_gathered(own_x)
    active = prepare(whole_x, chan_sum, chan_square, total_count, first_gain, first_bias, at_start)
    hidden_one = local_conv(active, first_kernel, frames_n).astype(jnp.bfloat16)
    whole_h = gather_channels(jnp.concatenate([past_small(hidden_one[-2:]), hidden_one], 0))
    own_h = whole_h[2:]
    second_sum, second_square = stats_gathered(own_h)
    active_two = prepare(
        whole_h, second_sum, second_square, total_count, second_gain, second_bias, at_start
    )
    residual = lax.dynamic_slice_in_dim(own_x, offset, chan_part, 3)
    summed = (
        residual.astype(jnp.float32) + local_conv(active_two, second_kernel, frames_n)
    ).astype(jnp.bfloat16)
    expanded = jnp.einsum(
        "thwc,cd->thwd", gather_channels(summed), expand_kernel, preferred_element_type=jnp.float32
    ).astype(jnp.bfloat16)
    arrived = lax.all_to_all(expanded, "rows", split_axis=1, concat_axis=3, tiled=True)
    return depth_space(arrived)


def solution(mesh):
    return jax.shard_map(
        shards,
        mesh=mesh,
        in_specs=(
            P("tm", "rows", None, None),
            P(),
            P(),
            P(),
            P(),
            P(None, None, None, "rows", None),
            P(None, None, None, "rows", None),
            P(None, "rows"),
        ),
        out_specs=P("tm", "rows", None, None),
        check_vma=False,
    )
```

profile of v0, /device:TPU:2, one launch (start us, length us, event | category | flops | bytes accessed | tf_op | source)
XLA Modules:
  0.0 681.4 jit_solution(3440813985927339558)
XLA Ops:
  6.5 0.9 slice.342
  7.4 1.9 collective-permute-start
  9.3 5.6 collective-permute-done
  14.9 1.5 pad_maximum_fusion.1
  16.6 84.9 %all-gather.4.cloned.1.call-done = bf16[5,16,16,768]{3,2,1,0:T(8,128)(2,1)} async-done(((bf16[5,1,16,768]{3,2,1,0:T(8,128)(2,1)}), bf16[5,16,16,768]{3,2,1,0:T(8,128)(2,1)}) %all-gather.4.cloned.1.call-update) | async-done | bytes 1966096 | tf_op jit(solution)/shard_map/all_gather | solution.py:20
  101.4 1.6 convert_reduce_fusion.1
  103.2 53.0 %all-reduce.3 = (f32[32,24]{1,0:T(8,128)S(1)}, f32[32,24]{1,0:T(8,128)S(1)}) all-reduce(f32[32,24]{1,0:T(8,128)S(1)} %reshape.33, f32[32,24]{1,0:T(8,128)S(1)} %reshape.32), channel_id=1, replica_groups=mesh['tm'=16,'rows'=16] {'tm'}, use_global_device_ids=true, to_apply=%region_4.0 | all-reduce | flops 1536 | bytes 12288 | tf_op jit(solution)/shard_map/psum | solution.py:34
  156.7 3.2 fusion.4
  160.4 0.5 convolution_add_fusion.45
  160.9 0.5 convolution_add_fusion.44
  161.3 0.5 convolution_add_fusion.43
  161.8 0.5 convolution_add_fusion.48
  162.3 0.5 convolution_add_fusion.42
  162.7 0.5 convolution_add_fusion.41
  163.7 0.5 convolution_add_fusion.39
  164.1 0.5 convolution_add_fusion.38
  165.1 0.5 convolution_add_fusion.36
  165.5 0.5 convolution_add_fusion.35
  166.0 0.5 convolution_add_fusion.47
  166.5 0.5 convolution_add_fusion.34
  167.0 0.5 convolution_add_fusion.33
  167.9 0.5 convolution_add_fusion.31
  168.4 0.5 convolution_add_fusion.30
  169.3 0.5 convolution_add_fusion.28
  169.8 0.5 convolution_add_fusion.27
  170.2 0.5 convolution_add_fusion.46
  170.7 0.5 convolution_add_fusion.26
  171.2 0.5 convolution_add_fusion.25
  172.1 0.9 fusion.16
  173.1 1.9 collective-permute-start.1
  175.0 6.5 collective-permute-done.1
  181.5 1.7 copy.13
  183.3 207.7 %all-gather.6.cloned.1.call-done = bf16[5,16,16,768]{2,1,0,3:T(8,128)(2,1)} async-done(((bf16[5,16,16,48]{2,1,0,3:T(8,128)(2,1)}), bf16[5,16,16,768]{2,1,0,3:T(8,128)(2,1)}) %all-gather.6.cloned.1.call-update) | async-done | bytes 1966096 | tf_op jit(solution)/shard_map/all_gather | solution.py:24
  390.9 10.1 %convert_reduce_fusion = (f32[768]{0:T(1024)S(1)}, f32[768]{0:T(1024)S(1)}) fusion(bf16[5,16,16,768]{2,1,0,3:T(8,128)(2,1)} %all-gather.6.cloned.1.call-done), kind=kLoop, calls=%fused_computation.1 | loop fusion | flops 2357760 | bytes 1185792 | tf_op jit(solution)/shard_map/reduce_sum | solution.py:29
  401.2 55.5 %all-reduce.2 = (f32[32,24]{1,0:T(8,128)S(1)}, f32[32,24]{1,0:T(8,128)S(1)}) all-reduce(f32[32,24]{1,0:T(8,128)S(1)} %reshape.35, f32[32,24]{1,0:T(8,128)S(1)} %reshape.34), channel_id=1, replica_groups=mesh['tm'=16,'rows'=16] {'tm'}, use_global_device_ids=true, to_apply=%region_10.11 | all-reduce | flops 1536 | bytes 12288 | tf_op jit(solution)/shard_map/psum | solution.py:34
  457.2 12.9 %copy.14 = bf16[5,16,16,768]{3,2,1,0:T(8,128)(2,1)S(1)} copy(bf16[5,16,16,768]{2,1,0,3:T(8,128)(2,1)} %all-gather.6.cloned.1.call-done) | data formatting | bytes 3932160 | tf_op jit(solution)/shard_map/all_gather | solution.py:24
  470.1 1.5 fusion.5
  473.0 0.5 fusion.14
  473.5 0.5 convolution_add_fusion.22
  473.9 0.5 convolution_add_fusion.21
  474.4 0.5 fusion.9
  474.9 0.5 convolution_add_fusion.19
  475.4 0.5 convolution_add_fusion.18
  476.3 0.5 convolution_add_fusion.16
  476.8 0.5 convolution_add_fusion.15
  477.7 0.5 convolution_add_fusion.13
  478.2 0.5 fusion.10
  478.6 0.5 convolution_add_fusion.11
  479.1 0.5 convolution_add_fusion.10
  480.1 0.5 convolution_add_fusion.8
  480.5 0.5 convolution_add_fusion.7
  481.5 0.5 convolution_add_fusion.5
  481.9 0.5 fusion.11
  482.4 0.5 convolution_add_fusion.3
  482.9 0.5 convolution_add_fusion.2
  483.8 0.8 slice-done
  484.6 0.7 fusion.15
  485.3 1.3 copy.15
  486.6 140.8 %all-gather.8.cloned.1.call-done = bf16[3,16,16,768]{2,1,0,3:T(8,128)(2,1)} async-done(((bf16[3,16,16,48]{2,1,0,3:T(8,128)(2,1)}), bf16[3,16,16,768]{2,1,0,3:T(8,128)(2,1)}) %all-gather.8.cloned.1.call-update) | async-done | bytes 1179664 | tf_op jit(solution)/shard_map/all_gather | solution.py:24
  627.4 6.5 fusion.6
  634.0 25.4 %all_to_all.15 = bf16[3,16,16,384]{3,2,0,1:T(8,128)(2,1)S(1)} all-to-all(bf16[3,16,16,384]{3,2,0,1:T(8,128)(2,1)S(1)} %copy.17), channel_id=1, replica_groups=mesh['tm'=16,'rows'=16] {'rows'}, dimensions={1} | all-to-all | bytes 1179648 | tf_op jit(solution)/shard_map/all_to_all | solution.py:118
  659.4 3.3 copy.18
  662.7 11.0 %copy.19 = bf16[3,3,1,2,16,2,512]{6,3,5,4,1,0,2:T(2,128)(2,1)S(1)} copy(bf16[3,3,1,2,16,2,512]{4,5,3,1,6,0,2:T(2,128)(2,1)} %bitcast.396) | data formatting | bytes 1179648 | tf_op jit(solution)/shard_map/transpose | solution.py:79
  673.7 0.9 copy.20
  (53 shorter events, 8.1 us)
Async XLA Ops:
  6.5 620.9 %copy-start = (bf16[768,384]{1,0:T(8,128)(2,1)S(1)}, bf16[768,384]{1,0:T(8,128)(2,1)}, u32[]{:S(2)}) copy-start(bf16[768,384]{1,0:T(8,128)(2,1)} %param.15) | copy-start | bytes 1769476
  6.5 94.9 %all-gather.4.cloned.1.call-start = ((), (), s32[]{:S(2)}) async-start(), calls=%async_computation.1 | async-start | bytes 2088960 | tf_op jit(solution)/shard_map/all_gather | solution.py:20
  7.4 7.5 %collective-permute-start = (bf16[2,1,16,768]{3,2,1,0:T(8,128)(2,1)S(1)}, bf16[2,1,16,768]{3,2,1,0:T(8,128)(2,1)S(1)}, u32[]{:S(2)}, u32[]{:S(2)}) collective-permute-start(bf16[2,1,16,768]{3,2,1,0:T(8,128)(2,1)S(1)} %slice.342), channel_id=1, source_target_pairs={{0,16},{16,32},{32,48},{48,64},{64,80},{80,96},{96,112},{112,128},... | collective-permute-start | bytes 147464 | tf_op jit(solution)/shard_map/ppermute | solution.py:12
  16.5 374.5 %all-gather.6.cloned.1.call-start = ((), (), s32[]{:S(2)}) async-start(), calls=%async_computation.2 | async-start | bytes 16711680 | tf_op jit(solution)/shard_map/all_gather | solution.py:24
  156.7 3.2 copy-start.1
  173.1 8.4 %collective-permute-start.1 = (bf16[2,16,16,48]{3,2,1,0:T(8,128)(2,1)S(1)}, bf16[2,16,16,48]{3,2,1,0:T(8,128)(2,1)S(1)}, u32[]{:S(2)}, u32[]{:S(2)}) collective-permute-start(bf16[2,16,16,48]{3,2,1,0:T(8,128)(2,1)S(1)} %slice.455), channel_id=1, source_target_pairs={{0,16},{16,32},{32,48},{48,64},{64,80},{80,96},{96,112},{112,128},... | collective-permute-start | bytes 147464 | tf_op jit(solution)/shard_map/ppermute | solution.py:12
  183.2 444.2 %all-gather.8.cloned.1.call-start = ((), (), s32[]{:S(2)}) async-start(), calls=%async_computation.3 | async-start | bytes 10027008 | tf_op jit(solution)/shard_map/all_gather | solution.py:24
  457.2 12.9 %copy-start.3 = (f32[768]{0:T(1024)S(1)}, f32[768]{0:T(1024)}, u32[]{:S(2)}) copy-start(f32[768]{0:T(1024)} %param.12) | copy-start | bytes 9220
  457.2 12.9 %copy-start.4 = (f32[768]{0:T(1024)S(1)}, f32[768]{0:T(1024)}, u32[]{:S(2)}) copy-start(f32[768]{0:T(1024)} %param.11) | copy-start | bytes 9220
  470.1 1.6 copy-start.2
  483.4 1.3 slice-start
Sparse Core Ops, SparseCore 0:
  16.6 84.7 all-gather.3
  183.3 207.5 all-gather.5
  486.8 140.6 all-gather.7
where the time goes:
time: 691 us; the launch traced here: 681 us
  waiting for transfers between devices  445 us (64%)
  blocking collectives  134 us (19%)
  local copies, waits for them, and re-layouts  33.8 us (5%)
  matrix products  32.2 us (5%)
  other arithmetic  18.4 us (3%)
  between operations  13.8 us (2%)
    all_gather x2, waiting for transfers between devices, gather_channels(): return lax.all_gather(field, 'rows', axis=3, tiled=True)  348 us
    psum x2, blocking collectives, stats_gathered(): return lax.psum((chan_sum, chan_square), 'tm')  108 us
    all_gather x1, waiting for transfers between devices, gather_rows(): return lax.all_gather(field, 'rows', axis=1, tiled=True)  84.9 us
    dot_general x54, matrix products, local_conv(): jnp.einsum('thwc,dc->thwd', window, kernel[tap_time, tap_row, tap_col], p...  25.7 us
    all_to_all x1, blocking collectives, shards(): lax.all_to_all(expanded, 'rows', split_axis=1, concat_axis=3, tiled=True)  25.4 us
  transfers between devices with their start and end apart: 5, of which 5 were waited for; matrix products, arithmetic and copies ran while one was open for 0% of the time, Pallas kernels for 0%

commit v1 on v0

v1 whole, which is shorter than its diff:
```python
import jax
import jax.numpy as jnp
from jax import lax
from jax.experimental import pallas as pl
from jax.experimental.pallas import tpu as pltpu
from jax.sharding import PartitionSpec as P

MESH = pl.DeviceIdType.MESH
BF16 = jnp.bfloat16
F32 = jnp.float32
HIGH = lax.Precision.HIGHEST

CH = 768
OWN = 48
FRAMES = 3
PLANE = 256
TAPS = 9 * OWN
COUNT = 48 * 16 * 16 * 24
NT = (((1,), (1,)), ((), ()))


def iota(shape, axis):
    return lax.broadcasted_iota(jnp.int32, shape, axis)


def loop(count, body):
    def step(i, carry):
        body(i)
        return carry

    lax.fori_loop(0, count, step, 0)


def push(src, dst, send_sem, recv_sem, device):
    pltpu.make_async_remote_copy(
        src_ref=src,
        dst_ref=dst,
        send_sem=send_sem,
        recv_sem=recv_sem,
        device_id=device,
        device_id_type=MESH,
    ).start()


def await_recv(ref, sem):
    pltpu.make_async_copy(ref, ref, sem).wait()


def combine(taps):
    lane = iota((OWN, PLANE), 1)
    column = lane & 15
    total = None
    for tap_row in range(3):
        base = tap_row * 3 * OWN
        line = taps[base + OWN : base + 2 * OWN]
        line += jnp.where(column != 0, pltpu.roll(taps[base : base + OWN], 1, 1), 0.0)
        line += jnp.where(
            column != 15, pltpu.roll(taps[base + 2 * OWN : base + 3 * OWN], PLANE - 1, 1), 0.0
        )
        if tap_row == 0:
            line = jnp.where(lane >= 16, pltpu.roll(line, 16, 1), 0.0)
        elif tap_row == 2:
            line = jnp.where(lane < PLANE - 16, pltpu.roll(line, PLANE - 16, 1), 0.0)
        total = line if total is None else total + line
    return total


def silu(value):
    return value * jax.nn.sigmoid(value)


def group_matrix(shape, group_axis):
    channel = iota(shape, 1 - group_axis)
    return ((channel * 2731) >> 16 == iota(shape, group_axis)).astype(F32)


def kernel(
    x_ref,
    gain1_ref,
    bias1_ref,
    gain2_ref,
    bias2_ref,
    w1_hbm,
    w2_hbm,
    ek_ref,
    out_ref,
    w1,
    w2,
    xg,
    act,
    hg,
    ekt,
    taps,
    hid,
    halo_out,
    halo_in,
    stat_rows,
    stat_tm,
    stat_two,
    pack,
    sg,
    sem_w,
    sx_send,
    sx,
    sh_send,
    sh,
    se_send,
    se,
    sstat_send,
    sstat,
    shalo_send,
    shalo,
    sg_send,
    sg_recv,
):
    t = lax.axis_index("tm")
    r = lax.axis_index("rows")
    xh = r // 8
    z = lax.rem(r, 8)
    half = lax.rem(t, 2)

    def slot(other, distance):
        line = 1 - xh if other else xh
        return line * 8 + lax.rem(z + distance + 8, 8)

    up = (t, slot(False, 1))
    down = (t, slot(False, -1))
    partner = (t, slot(True, 0))
    sibling = (t + 1 - 2 * half, r)

    load1 = pltpu.make_async_copy(w1_hbm, w1, sem_w.at[0])
    load2 = pltpu.make_async_copy(w2_hbm, w2, sem_w.at[1])
    load1.start()
    load2.start()

    barrier = pltpu.get_barrier_semaphore()

    def greet(i):
        pl.semaphore_signal(
            barrier, inc=1, device_id=(t, lax.rem(r + 1 + i, 16)), device_id_type=MESH
        )
        pl.semaphore_signal(
            barrier, inc=1, device_id=(lax.rem(t + 1 + i, 16), r), device_id_type=MESH
        )

    loop(15, greet)

    for frame in range(FRAMES):
        xg[pl.ds(pl.multiple_of(frame * PLANE + r * 16, 16), 16)] = x_ref[
            frame * 16 : frame * 16 + 16
        ]
    own = x_ref[...].astype(F32)
    row8 = iota((8, CH), 0)
    sums = jnp.where(
        row8 == 0,
        jnp.sum(own, axis=0, keepdims=True),
        jnp.where(row8 == 1, jnp.sum(own * own, axis=0, keepdims=True), 0.0),
    )
    stat_rows[r] = jnp.dot(
        sums, group_matrix((CH, 128), 1), precision=HIGH, preferred_element_type=F32
    )

    @pl.when(t == 0)
    def _():
        halo_in[...] = jnp.zeros_like(halo_in)

    pl.semaphore_wait(barrier, 30)

    def exchange_rows(i):
        push(
            stat_rows.at[r],
            stat_rows.at[r],
            sstat_send.at[0],
            sstat.at[0],
            (t, lax.rem(r + 1 + i, 16)),
        )

    loop(15, exchange_rows)

    def ring(view, send_sem, sems, after_start):
        def send(which, frame, device):
            ref = view(which, frame)
            push(ref, ref, send_sem, sems.at[which, frame], device)

        def wait(which, frame):
            await_recv(view(which, frame), sems.at[which, frame])

        def start(i):
            frame = FRAMES - 1 - i
            for device in (partner, up, down):
                send(r, frame, device)

        def first(i):
            frame = FRAMES - 1 - i
            which = slot(True, 0)
            wait(which, frame)
            send(which, frame, up)
            send(which, frame, down)

        loop(FRAMES, start)
        after_start()
        loop(FRAMES, first)
        for step in range(1, 5):

            def forward(i, step=step):
                frame = FRAMES - 1 - i
                for other in (False, True):
                    for sign in (-1, 1):
                        last = 4 if (sign == -1) == (not other) else 3
                        if step > last:
                            continue
                        which = slot(other, sign * step)
                        wait(which, frame)
                        if step < last:
                            send(which, frame, up if sign == -1 else down)

            loop(FRAMES, forward)

    def view_x(which, frame):
        return xg.at[pl.ds(pl.multiple_of(frame * PLANE + which * 16, 16), 16)]

    def view_h(which, frame):
        return hg.at[pl.ds(pl.multiple_of(frame * CH + which * OWN, 16), OWN)]

    def exchange_tm():
        await_recv(stat_rows.at[pl.ds(0, 15)], sstat.at[0])
        stat_tm[t] = jnp.sum(stat_rows[...], axis=0)

        def send(i):
            push(
                stat_tm.at[t],
                stat_tm.at[t],
                sstat_send.at[1],
                sstat.at[1],
                (lax.rem(t + 1 + i, 16), r),
            )

        loop(15, send)
        row = iota((384, 384), 0)
        place = (iota((384, 384), 1) == 12 * (row & 31) + (row >> 5)).astype(BF16)
        turned = lax.dot_general(place, ek_ref[...], NT, preferred_element_type=F32).astype(BF16)
        for sub in range(12):
            ekt[sub, pl.ds(pl.multiple_of(r * 32, 32), 32)] = turned[sub * 32 : sub * 32 + 32]

    ring(view_x, sx_send, sx, exchange_tm)

    def view_e(part, which):
        return ekt.at[pl.ds(part * 6, 6), pl.ds(pl.multiple_of(which * 32, 32), 32)]

    def send_e(which, device):
        ref = view_e(half, which)
        push(ref, ref, se_send, se.at[half, which], device)

    def expand_start():
        for device in (up, down, partner):
            send_e(r, device)

    def expand_step(step):
        for sign, last in ((-1, 4), (1, 3)):
            if step > last:
                continue
            which = slot(False, sign * step)
            await_recv(view_e(half, which), se.at[half, which])
            if step < last:
                send_e(which, up if sign == -1 else down)
            send_e(which, partner)
            send_e(which, sibling)

    def expand_across(i):
        which = (1 - xh) * 8 + i
        await_recv(view_e(half, which), se.at[half, which])
        send_e(which, sibling)

    def expand_last(i):
        which = lax.rem(r + 1 + i, 16)
        await_recv(view_e(1 - half, which), se.at[1 - half, which])

    expand_start()

    await_recv(stat_tm.at[pl.ds(0, 15)], sstat.at[1])
    averages = jnp.sum(stat_tm[...], axis=0) * (1.0 / COUNT)
    mean, square = averages[0:1], averages[1:2]
    inverse = lax.rsqrt(square - mean * mean + 1e-06)
    row8 = iota((8, 128), 0)
    spreads = jnp.where(row8 == 0, mean, jnp.where(row8 == 1, inverse, 0.0))
    per_channel = jnp.dot(
        spreads, group_matrix((128, CH), 0), precision=HIGH, preferred_element_type=F32
    )
    mean = per_channel[0:1]
    scale = per_channel[1:2] * gain1_ref[...]
    bias = bias1_ref[...]

    def activate(i):
        at = pl.ds(pl.multiple_of(i * 32, 32), 32)
        act[at] = silu((xg[at].astype(F32) - mean) * scale + bias).astype(BF16)

    loop(FRAMES * PLANE // 32, activate)

    to_next = (lax.rem(t + 1, 16), r)

    def convolve(weights, product, which, between):
        taps[...] = jnp.zeros_like(taps)

        def step(i, first):
            frame = first - i // 3
            tap_time = lax.rem(i, 3)
            rows = weights[pl.ds(pl.multiple_of(tap_time * TAPS, 16), TAPS)]
            taps[frame + 2 - tap_time] += product(rows, frame)

        loop(6, lambda i: step(i, 2))
        halo_out[which, 0] = combine(taps[3])
        halo_out[which, 1] = combine(taps[4])

        @pl.when(t < 15)
        def _():
            push(
                halo_out.at[which],
                halo_in.at[which],
                shalo_send.at[which],
                shalo.at[which],
                to_next,
            )

        loop(3, lambda i: step(i, 0))
        results = [combine(taps[frame]) for frame in range(FRAMES)]
        between()

        @pl.when(t > 0)
        def _():
            await_recv(halo_in.at[which], shalo.at[which])

        results[0] = results[0] + halo_in[which, 0]
        results[1] = results[1] + halo_in[which, 1]
        return results

    def product_one(rows, frame):
        at = pl.ds(pl.multiple_of(frame * PLANE, PLANE), PLANE)
        return lax.dot_general(rows, act[at], NT, preferred_element_type=F32)

    def product_two(rows, frame):
        at = pl.ds(pl.multiple_of(frame * CH, CH), CH)
        return jnp.dot(rows, hg[at], preferred_element_type=F32)

    load1.wait()
    hidden = [
        value.astype(BF16).astype(F32)
        for value in convolve(w1, product_one, 0, lambda: expand_step(1))
    ]

    added = hidden[0] + hidden[1] + hidden[2]
    squared = hidden[0] * hidden[0] + hidden[1] * hidden[1] + hidden[2] * hidden[2]
    lines = []
    for field in (added, squared):
        field = field[:, :128] + field[:, 128:]
        for group in range(2):
            lines.append(jnp.sum(field[group * 24 : group * 24 + 24], axis=0, keepdims=True))
    message = jnp.zeros((8, 128), F32)
    for i, line in enumerate(lines):
        message = jnp.where(row8 == i, line, message)
    stat_two[t] = message

    def exchange_two(i):
        push(
            stat_two.at[t],
            stat_two.at[t],
            sstat_send.at[2],
            sstat.at[2],
            (lax.rem(t + 1 + i, 16), r),
        )

    loop(15, exchange_two)
    pick = iota((OWN, CH), 1) == r * OWN + iota((OWN, CH), 0)
    gain = jnp.sum(jnp.where(pick, gain2_ref[...], 0.0), axis=1, keepdims=True)
    bias = jnp.sum(jnp.where(pick, bias2_ref[...], 0.0), axis=1, keepdims=True)
    await_recv(stat_two.at[pl.ds(0, 15)], sstat.at[2])
    averages = jnp.sum(jnp.sum(stat_two[...], axis=0), axis=1, keepdims=True) * (1.0 / COUNT)
    group = iota((OWN, 1), 0) < 24
    mean = jnp.where(group, averages[0:1], averages[1:2])
    square = jnp.where(group, averages[2:3], averages[3:4])
    scale = lax.rsqrt(square - mean * mean + 1e-06) * gain
    for frame in range(FRAMES):
        at = pl.ds(pl.multiple_of(frame * CH + r * OWN, 16), OWN)
        hg[at] = silu((hidden[frame] - mean) * scale + bias).astype(BF16)

    ring(view_h, sh_send, sh, lambda: expand_step(2))

    load2.wait()
    expand_step(3)
    sums = convolve(w2, product_two, 1, lambda: expand_step(4))
    pick = pick.astype(BF16)
    for frame in range(FRAMES):
        residual = lax.dot_general(
            pick, xg[frame * PLANE : (frame + 1) * PLANE], NT, preferred_element_type=F32
        )
        hid[frame] = (sums[frame] + residual).astype(BF16).astype(F32)

    lane = iota((OWN, 128), 1)
    for part in range(2):
        for line in range(8):
            total = jnp.zeros((OWN, 128), F32)
            for frame in range(FRAMES):
                moved = pltpu.roll(
                    hid[frame, :, part * 128 : part * 128 + 128], (16 * (frame - line)) % 128, 1
                )
                total = jnp.where(lane >> 4 == frame, moved, total)
            pack[part * 8 + line] = total.astype(BF16)
    mine = pl.ds(pl.multiple_of(r * OWN, 16), OWN)
    sg[mine] = pack[r]

    def to_rows(i):
        other = lax.rem(r + 1 + i, 16)
        push(pack.at[other], sg.at[mine], sg_send, sg_recv, (t, other))

    loop(15, to_rows)
    loop(8, expand_across)
    loop(15, expand_last)
    await_recv(sg.at[pl.ds(0, 15 * OWN)], sg_recv)

    lane = iota((128, 128), 1)
    source = ((lane >> 5) << 4) + ((lane & 31) >> 1)
    double = ((iota((128, 128), 0) == source) & (lane < 96)).astype(BF16)
    doubled = jnp.dot(sg[...], double, preferred_element_type=F32).astype(BF16)
    even = (iota((512, 128), 1) & 1) == 0

    def expand(i):
        one = jnp.dot(ekt[2 * i], doubled, preferred_element_type=F32)
        two = jnp.dot(ekt[2 * i + 1], doubled, preferred_element_type=F32)
        turned = jnp.where(even, one, two).T.astype(BF16)
        for frame in range(FRAMES):
            out_ref[3 * frame + i // 2, lax.rem(i, 2)] = turned[frame * 32 : frame * 32 + 32]

    loop(6, expand)

    await_recv(xg.at[pl.ds(0, 15 * 48)], sx_send)
    await_recv(hg.at[pl.ds(0, 15 * 144)], sh_send)
    for _ in range(2):
        await_recv(ekt.at[pl.ds(0, 6), pl.ds(0, 480)], se_send)
    await_recv(stat_rows.at[pl.ds(0, 15)], sstat_send.at[0])
    await_recv(stat_tm.at[pl.ds(0, 15)], sstat_send.at[1])
    await_recv(stat_two.at[pl.ds(0, 15)], sstat_send.at[2])
    await_recv(sg.at[pl.ds(0, 15 * OWN)], sg_send)

    @pl.when(t < 15)
    def _():
        await_recv(halo_out.at[0], shalo_send.at[0])
        await_recv(halo_out.at[1], shalo_send.at[1])


def shards(
    latents,
    first_gain,
    first_bias,
    second_gain,
    second_bias,
    first_kernel,
    second_kernel,
    expand_kernel,
):
    vmem = pl.BlockSpec(memory_space=pltpu.VMEM)
    anywhere = pl.BlockSpec(memory_space=pl.ANY)
    dma = pltpu.SemaphoreType.DMA
    return pl.pallas_call(
        kernel,
        out_shape=jax.ShapeDtypeStruct((9, 2, 32, 512), BF16),
        in_specs=[vmem] * 5 + [anywhere] * 2 + [vmem],
        out_specs=vmem,
        scratch_shapes=[
            pltpu.VMEM((27 * OWN, CH), BF16),
            pltpu.VMEM((27 * OWN, CH), BF16),
            pltpu.VMEM((FRAMES * PLANE, CH), BF16),
            pltpu.VMEM((FRAMES * PLANE, CH), BF16),
            pltpu.VMEM((FRAMES * CH, PLANE), BF16),
            pltpu.VMEM((12, 512, CH), BF16),
            pltpu.VMEM((5, TAPS, PLANE), F32),
            pltpu.VMEM((FRAMES, OWN, PLANE), F32),
            pltpu.VMEM((2, 2, OWN, PLANE), F32),
            pltpu.VMEM((2, 2, OWN, PLANE), F32),
            pltpu.VMEM((16, 8, 128), F32),
            pltpu.VMEM((16, 8, 128), F32),
            pltpu.VMEM((16, 8, 128), F32),
            pltpu.VMEM((16, OWN, 128), BF16),
            pltpu.VMEM((CH, 128), BF16),
            dma((2,)),
            dma,
            dma((16, FRAMES)),
            dma,
            dma((16, FRAMES)),
            dma,
            dma((2, 16)),
            dma((3,)),
            dma((3,)),
            dma((2,)),
            dma((2,)),
            dma,
            dma,
        ],
        compiler_params=pltpu.CompilerParams(
            collective_id=0, has_side_effects=True, vmem_limit_bytes=48 << 20
        ),
        name="block",
    )(
        latents.reshape(48, CH),
        first_gain.reshape(1, CH),
        first_bias.reshape(1, CH),
        second_gain.reshape(1, CH),
        second_bias.reshape(1, CH),
        first_kernel.reshape(27 * OWN, CH),
        second_kernel.reshape(27 * OWN, CH),
        expand_kernel,
    )


def solution(mesh):
    return jax.shard_map(
        shards,
        mesh=mesh,
        in_specs=(
            P("tm", "rows", None, None),
            P(),
            P(),
            P(),
            P(),
            P(None, None, None, "rows", None),
            P(None, None, None, "rows", None),
            P(None, "rows"),
        ),
        out_specs=P("tm", "rows", None, None),
        check_vma=False,
    )
```

time: 691 us -> 117 us (0.17)
  the two profiles are of different devices: /device:TPU:2 before, /device:TPU:1 now
where the time goes in v1:
time: 117 us
  Pallas kernels  108 us (92%)
  local copies, waits for them, and re-layouts  8.63 us (7%)
    pallas_call x1, Pallas kernels, shards(): pl.pallas_call(kernel, out_shape=jax.ShapeDtypeStruct((9, 2, 32, 512), BF...  108 us
    unnamed x9, local copies, waits for them, and re-layouts  5.87 us

profile of v1, /device:TPU:1, one launch (start us, length us, event | category | flops | bytes accessed | tf_op | source)
XLA Modules:
  0.0 116.7 jit_solution(4122540993447711913)
XLA Ops:
  0.0 0.7 reshape.22.gain1_ref
  0.7 0.7 reshape.23.bias1_ref
  1.4 0.7 reshape.24.gain2_ref
  2.1 0.7 reshape.25.bias2_ref
  2.8 0.0 copy-start
  2.8 1.6 %copy-done = bf16[3,3,3,48,768]{4,3,2,1,0:T(8,128)(2,1)S(1)} copy-done((bf16[3,3,3,48,768]{4,3,2,1,0:T(8,128)(2,1)S(1)}, bf16[3,3,3,48,768]{4,3,2,1,0:T(8,128)(2,1)}, u32[]{:S(2)}) %copy-start) | copy-done | bytes 1990680
  4.3 0.0 copy-start.1
  4.3 1.6 %copy-done.1 = bf16[3,3,3,48,768]{4,3,2,1,0:T(8,128)(2,1)S(1)} copy-done((bf16[3,3,3,48,768]{4,3,2,1,0:T(8,128)(2,1)S(1)}, bf16[3,3,3,48,768]{4,3,2,1,0:T(8,128)(2,1)}, u32[]{:S(2)}) %copy-start.1) | copy-done | bytes 1990680
  5.9 0.0 copy-start.2
  5.9 1.1 copy-done.2
  6.9 0.0 copy-start.3
  6.9 0.9 copy-done.3
  7.8 108.1 %block.1 = bf16[9,2,32,512]{3,2,1,0:T(8,128)(2,1)S(1)} custom-call(bf16[48,768]{1,0:T(8,128)(2,1)S(1)} %bitcast.5, f32[1,768]{1,0:T(1,128)S(1)} %reshape.22.gain1_ref, f32[1,768]{1,0:T(1,128)S(1)} %reshape.23.bias1_ref, f32[1,768]{1,0:T(1,128)S(1)} %reshape.24.gain2_ref, f32[1,768]{1,0:T(1,128)S(1)} %reshape.25.bias2_ref, bf16[1296,768]{1,0:T(8,128)(2,1)S(1)} %bitcast.3, ...), custom_call_target="tpu_custom_call" | custom-call | tf_op jit(solution)/shard_map/block/pallas_call | solution.py:462
  115.9 0.8 copy.10
Async XLA Ops:
  2.8 1.6 %copy-start = (bf16[3,3,3,48,768]{4,3,2,1,0:T(8,128)(2,1)S(1)}, bf16[3,3,3,48,768]{4,3,2,1,0:T(8,128)(2,1)}, u32[]{:S(2)}) copy-start(bf16[3,3,3,48,768]{4,3,2,1,0:T(8,128)(2,1)} %param.13) | copy-start | bytes 5971972
  4.3 1.6 %copy-start.1 = (bf16[3,3,3,48,768]{4,3,2,1,0:T(8,128)(2,1)S(1)}, bf16[3,3,3,48,768]{4,3,2,1,0:T(8,128)(2,1)}, u32[]{:S(2)}) copy-start(bf16[3,3,3,48,768]{4,3,2,1,0:T(8,128)(2,1)} %param.14) | copy-start | bytes 5971972
  5.9 1.1 copy-start.2
  6.9 0.9 copy-start.3

commit v2 on v1

v2 whole, which is shorter than its diff:
```python
import jax
import jax.numpy as jnp
from jax import lax
from jax.experimental import pallas as pl
from jax.experimental.pallas import tpu as pltpu
from jax.sharding import PartitionSpec as P

MESH = pl.DeviceIdType.MESH
BF16 = jnp.bfloat16
F32 = jnp.float32
HIGH = lax.Precision.HIGHEST

CH = 768
OWN = 48
FRAMES = 3
PLANE = 256
TAPS = 9 * OWN
COUNT = 48 * 16 * 16 * 24
NT = (((1,), (1,)), ((), ()))


def iota(shape, axis):
    return lax.broadcasted_iota(jnp.int32, shape, axis)


def loop(count, body):
    def step(i, carry):
        body(i)
        return carry

    lax.fori_loop(0, count, step, 0)


def push(src, dst, send_sem, recv_sem, device):
    pltpu.make_async_remote_copy(
        src_ref=src,
        dst_ref=dst,
        send_sem=send_sem,
        recv_sem=recv_sem,
        device_id=device,
        device_id_type=MESH,
    ).start()


def await_recv(ref, sem):
    pltpu.make_async_copy(ref, ref, sem).wait()


def combine(taps):
    lane = iota((OWN, PLANE), 1)
    column = lane & 15
    total = None
    for tap_row in range(3):
        base = tap_row * 3 * OWN
        line = taps[base + OWN : base + 2 * OWN]
        line += jnp.where(column != 0, pltpu.roll(taps[base : base + OWN], 1, 1), 0.0)
        line += jnp.where(
            column != 15, pltpu.roll(taps[base + 2 * OWN : base + 3 * OWN], PLANE - 1, 1), 0.0
        )
        if tap_row == 0:
            line = jnp.where(lane >= 16, pltpu.roll(line, 16, 1), 0.0)
        elif tap_row == 2:
            line = jnp.where(lane < PLANE - 16, pltpu.roll(line, PLANE - 16, 1), 0.0)
        total = line if total is None else total + line
    return total


def silu(value):
    return value * jax.nn.sigmoid(value)


def group_matrix(shape, group_axis):
    channel = iota(shape, 1 - group_axis)
    return ((channel * 2731) >> 16 == iota(shape, group_axis)).astype(F32)


def kernel(
    x_hbm,
    gain1_ref,
    bias1_ref,
    gain2_ref,
    bias2_ref,
    w1_hbm,
    w2_hbm,
    ek_hbm,
    out_ref,
    x_ref,
    ek_ref,
    w1,
    w2,
    xg,
    act,
    hg,
    act_two,
    ekt,
    taps,
    results,
    hid,
    halo_out,
    halo_in,
    stat_rows,
    stat_tm,
    stat_two,
    norms,
    gain_columns,
    bias_columns,
    across,
    pack,
    sg,
    sem_w,
    sx_send,
    sx,
    sh_send,
    sh,
    se_send,
    se,
    sstat_send,
    sstat,
    shalo_send,
    shalo,
    sg_send,
    sg_recv,
    so_send,
    so_recv,
):
    t = lax.axis_index("tm")
    r = lax.axis_index("rows")
    xh = r // 8
    z = lax.rem(r, 8)
    half = lax.rem(t, 2)

    def slot(other, distance):
        line = 1 - xh if other else xh
        return line * 8 + lax.rem(z + distance + 8, 8)

    up = (t, slot(False, 1))
    down = (t, slot(False, -1))
    partner = (t, slot(True, 0))
    sibling = (t + 1 - 2 * half, r)

    load_x = pltpu.make_async_copy(x_hbm, x_ref, sem_w.at[0])
    load_e = pltpu.make_async_copy(ek_hbm, ek_ref, sem_w.at[1])
    load1 = pltpu.make_async_copy(w1_hbm, w1, sem_w.at[2])
    load2 = pltpu.make_async_copy(w2_hbm, w2, sem_w.at[3])
    for load in (load_x, load_e, load1, load2):
        load.start()

    barrier = pltpu.get_barrier_semaphore()

    def greet(i):
        pl.semaphore_signal(
            barrier, inc=1, device_id=(t, lax.rem(r + 1 + i, 16)), device_id_type=MESH
        )
        pl.semaphore_signal(
            barrier, inc=1, device_id=(lax.rem(t + 1 + i, 16), r), device_id_type=MESH
        )

    loop(15, greet)

    load_x.wait()
    for frame in range(FRAMES):
        xg[pl.ds(pl.multiple_of(frame * PLANE + r * 16, 16), 16)] = x_ref[
            frame * 16 : frame * 16 + 16
        ]
    own = x_ref[...].astype(F32)
    row8 = iota((8, CH), 0)
    sums = jnp.where(
        row8 == 0,
        jnp.sum(own, axis=0, keepdims=True),
        jnp.where(row8 == 1, jnp.sum(own * own, axis=0, keepdims=True), 0.0),
    )
    stat_rows[r] = jnp.dot(
        sums, group_matrix((CH, 128), 1), precision=HIGH, preferred_element_type=F32
    )

    @pl.when(t == 0)
    def _():
        halo_in[...] = jnp.zeros_like(halo_in)

    pl.semaphore_wait(barrier, 30)

    def exchange_rows(i):
        push(
            stat_rows.at[r],
            stat_rows.at[r],
            sstat_send.at[0],
            sstat.at[0],
            (t, lax.rem(r + 1 + i, 16)),
        )

    loop(15, exchange_rows)

    plan = [
        (False, 0, ("x", 2, -2, 1, -1)),
        (False, -2, (2, 1, "x")),
        (False, 2, (-1, "x")),
        (False, -1, ("x",)),
        (False, 1, ("x",)),
        (False, -3, ("x",)),
        (False, 3, ("x",)),
        (False, -4, ("x",)),
    ] + [(True, distance, ()) for distance in (0, -2, 2, -1, 1, -3, 3, -4)]

    def ring(view, send_sem, sems, hooks):
        for place, (other, distance, targets) in enumerate(plan):
            which = slot(other, distance)
            devices = [partner if to == "x" else (t, slot(False, to)) for to in targets]

            def piece(i, which=which, devices=devices, place=place):
                frame = FRAMES - 1 - i
                ref = view(which, frame)
                if place:
                    await_recv(ref, sems.at[which, frame])
                for device in devices:
                    push(ref, ref, send_sem, sems.at[which, frame], device)

            loop(FRAMES, piece)
            if place in hooks:
                hooks[place]()

    def view_x(which, frame):
        return xg.at[pl.ds(pl.multiple_of(frame * PLANE + which * 16, 16), 16)]

    def view_h(which, frame):
        return hg.at[pl.ds(pl.multiple_of(frame * CH + which * OWN, 16), OWN)]

    def exchange_tm():
        await_recv(stat_rows.at[pl.ds(0, 15)], sstat.at[0])
        stat_tm[t] = jnp.sum(stat_rows[...], axis=0)

        def send(i):
            push(
                stat_tm.at[t],
                stat_tm.at[t],
                sstat_send.at[1],
                sstat.at[1],
                (lax.rem(t + 1 + i, 16), r),
            )

        loop(15, send)

    def expand_prepare():
        load_e.wait()
        row = iota((384, 384), 0)
        place = (iota((384, 384), 1) == 12 * (row & 31) + (row >> 5)).astype(BF16)
        turned = lax.dot_general(place, ek_ref[...], NT, preferred_element_type=F32).astype(BF16)
        for sub in range(12):
            ekt[sub, pl.ds(pl.multiple_of(z * 32, 32), 32)] = turned[sub * 32 : sub * 32 + 32]
        expand_start()

    def view_e(part, which):
        return ekt.at[pl.ds(part * 6, 6), pl.ds(pl.multiple_of(which * 32, 32), 32)]

    def send_e(which, device):
        ref = view_e(half, which)
        push(ref, ref, se_send, se.at[half, which], device)

    def expand_start():
        send_e(z, up)
        send_e(z, down)

    def expand_step(step):
        for sign, last in ((-1, 4), (1, 3)):
            if step > last:
                continue
            which = lax.rem(z + sign * step + 8, 8)
            await_recv(view_e(half, which), se.at[half, which])
            if step < last:
                send_e(which, up if sign == -1 else down)
            send_e(which, sibling)

    def expand_last(i):
        which = lax.rem(z + 1 + i, 8)
        await_recv(view_e(1 - half, which), se.at[1 - half, which])

    ring(view_x, sx_send, sx, {0: expand_prepare, 7: exchange_tm})
    expand_step(1)

    await_recv(stat_tm.at[pl.ds(0, 15)], sstat.at[1])
    averages = jnp.sum(stat_tm[...], axis=0) * (1.0 / COUNT)
    mean, square = averages[0:1], averages[1:2]
    inverse = lax.rsqrt(square - mean * mean + 1e-06)
    row8 = iota((8, 128), 0)
    spreads = jnp.where(row8 == 0, mean, jnp.where(row8 == 1, inverse, 0.0))
    per_channel = jnp.dot(
        spreads, group_matrix((128, CH), 0), precision=HIGH, preferred_element_type=F32
    )
    mean = per_channel[0:1]
    scale = per_channel[1:2] * gain1_ref[...].reshape(1, CH)
    bias = bias1_ref[...].reshape(1, CH)

    def activate(i):
        at = pl.ds(pl.multiple_of(i * 32, 32), 32)
        act[at] = silu((xg[at].astype(F32) - mean) * scale + bias).astype(BF16)

    loop(FRAMES * PLANE // 32, activate)

    to_next = (lax.rem(t + 1, 16), r)

    def convolve(weights, product, which, between):
        def result(i):
            out_frame = 4 - i
            first = jnp.maximum(out_frame - 2, 0)
            taps[...] = jnp.zeros_like(taps)

            def step(frame, carry):
                tap_time = frame + 2 - out_frame
                rows = weights[pl.ds(pl.multiple_of(tap_time * TAPS, 16), TAPS)]
                taps[...] += product(rows, frame)
                return carry

            lax.fori_loop(first, jnp.minimum(out_frame, 2) + 1, step, 0)
            return combine(taps)

        def ahead(i):
            place = 1 - i
            halo_out[which, place] = result(i)

            @pl.when(t < 15)
            def _():
                push(
                    halo_out.at[which, place],
                    halo_in.at[which, place],
                    shalo_send.at[which],
                    shalo.at[which],
                    to_next,
                )

        def own(i):
            results[2 - i] = result(i + 2)

        loop(2, ahead)
        between()
        loop(3, own)

        @pl.when(t > 0)
        def _():
            await_recv(halo_in.at[which], shalo.at[which])

        return [
            results[0] + halo_in[which, 0],
            results[1] + halo_in[which, 1],
            results[2],
        ]

    def product_one(rows, frame):
        at = pl.ds(pl.multiple_of(frame * PLANE, PLANE), PLANE)
        return lax.dot_general(rows, act[at], NT, preferred_element_type=F32)

    def product_two(rows, frame):
        at = pl.ds(pl.multiple_of(frame * CH, CH), CH)
        return jnp.dot(rows, act_two[at], preferred_element_type=F32)

    load1.wait()
    hidden = [
        value.astype(BF16) for value in convolve(w1, product_one, 0, lambda: None)
    ]
    for frame in range(FRAMES):
        hg[pl.ds(pl.multiple_of(frame * CH + r * OWN, 16), OWN)] = hidden[frame]
    hidden = [value.astype(F32) for value in hidden]

    added = hidden[0] + hidden[1] + hidden[2]
    squared = hidden[0] * hidden[0] + hidden[1] * hidden[1] + hidden[2] * hidden[2]
    lines = []
    for field in (added, squared):
        field = field[:, :128] + field[:, 128:]
        for group in range(2):
            lines.append(jnp.sum(field[group * 24 : group * 24 + 24], axis=0, keepdims=True))
    message = jnp.zeros((8, 128), F32)
    for i, line in enumerate(lines):
        message = jnp.where(row8 == i, line, message)
    stat_two[t] = message

    def exchange_two(i):
        push(
            stat_two.at[t],
            stat_two.at[t],
            sstat_send.at[2],
            sstat.at[2],
            (lax.rem(t + 1 + i, 16), r),
        )

    def residuals():
        loop(15, exchange_two)
        pick = (iota((OWN, CH), 1) == r * OWN + iota((OWN, CH), 0)).astype(BF16)
        for frame in range(FRAMES):
            hid[frame] = lax.dot_general(
                pick, xg[frame * PLANE : (frame + 1) * PLANE], NT, preferred_element_type=F32
            )
        gain_columns[...] = jnp.broadcast_to(gain2_ref[...].reshape(1, CH), (128, CH)).T
        bias_columns[...] = jnp.broadcast_to(bias2_ref[...].reshape(1, CH), (128, CH)).T

    def spread_two():
        await_recv(stat_two.at[pl.ds(0, 15)], sstat.at[2])
        averages = jnp.sum(jnp.sum(stat_two[...], axis=0), axis=1, keepdims=True) * (1.0 / COUNT)
        averages = jnp.broadcast_to(averages, (8, 128))
        mean = averages[0:2]
        inverse = lax.rsqrt(averages[2:4] - mean * mean + 1e-06)
        norms[r] = jnp.where(
            row8 == 0,
            mean[0:1],
            jnp.where(row8 == 1, mean[1:2], jnp.where(row8 == 2, inverse[0:1], inverse[1:2])),
        )

        def send(i):
            push(
                norms.at[r],
                norms.at[r],
                sstat_send.at[3],
                sstat.at[3],
                (t, lax.rem(r + 1 + i, 16)),
            )

        loop(15, send)

    def after_line():
        spread_two()
        expand_step(2)

    ring(view_h, sh_send, sh, {0: residuals, 7: after_line})
    await_recv(norms.at[pl.ds(0, 15)], sstat.at[3])
    lower = iota((OWN, 128), 0) < 24

    def activate_two(i):
        source = lax.rem(i, 16)
        at = pl.ds(pl.multiple_of(i * OWN, 16), OWN)
        channels = pl.ds(pl.multiple_of(source * OWN, 16), OWN)
        norm = norms[source]
        mean = jnp.where(lower, norm[0:1], norm[1:2])
        scale = jnp.where(lower, norm[2:3], norm[3:4]) * gain_columns[channels]
        bias = bias_columns[channels]
        value = hg[at].astype(F32)
        act_two[at] = jnp.concatenate(
            [
                silu((value[:, part * 128 : part * 128 + 128] - mean) * scale + bias)
                for part in range(2)
            ],
            axis=1,
        ).astype(BF16)

    load2.wait()
    loop(16 * FRAMES, activate_two)
    sums = convolve(w2, product_two, 1, lambda: expand_step(3))
    for frame in range(FRAMES):
        hid[frame] = (sums[frame] + hid[frame]).astype(BF16).astype(F32)

    lane = iota((OWN, 128), 1)
    for line in range(8):
        total = jnp.zeros((OWN, 128), F32)
        for part in range(2):
            for frame in range(FRAMES):
                place = 3 * part + frame
                moved = pltpu.roll(
                    hid[frame, :, part * 128 : part * 128 + 128], (16 * (place - line)) % 128, 1
                )
                total = jnp.where(lane >> 4 == place, moved, total)
        pack[line] = total.astype(BF16)
    mine = pl.ds(pl.multiple_of(r * OWN, 16), OWN)
    sg[mine] = pack[z]

    def to_rows(i):
        other = lax.rem(r + 1 + i, 16)
        push(pack.at[lax.rem(other, 8)], sg.at[mine], sg_send, sg_recv, (t, other))

    loop(15, to_rows)
    expand_step(4)
    loop(7, expand_last)
    column = iota((128, PLANE), 1)
    second = (column >= 96).astype(jnp.int32)
    inside = column - 96 * second
    source = 48 * (second + xh - 2 * xh * second) + ((inside >> 5) << 4) + ((inside & 31) >> 1)
    double = ((iota((128, PLANE), 0) == source) & (column < 192)).astype(BF16)
    even = (iota((PLANE, PLANE), 1) & 1) == 0
    await_recv(sg.at[pl.ds(0, 15 * OWN)], sg_recv)

    doubled = jnp.dot(sg[...], double, preferred_element_type=F32).astype(BF16)
    own_half = pl.ds(pl.multiple_of(xh * 256, 256), 256)
    other_half = pl.ds(pl.multiple_of(256 - xh * 256, 256), 256)

    def expand(i):
        one = jnp.dot(ekt[2 * i], doubled, preferred_element_type=F32)
        two = jnp.dot(ekt[2 * i + 1], doubled, preferred_element_type=F32)
        turned = jnp.where(even, one, two).T.astype(BF16)
        tap_time, tap_row = i // 2, lax.rem(i, 2)
        for frame in range(FRAMES):
            out_ref[frame, tap_time, tap_row, :, own_half] = turned[frame * 32 : frame * 32 + 32]
            across[i, frame] = turned[96 + frame * 32 : 128 + frame * 32]
        push(
            across.at[i],
            out_ref.at[:, tap_time, tap_row, :, own_half],
            so_send,
            so_recv,
            partner,
        )

    loop(6, expand)
    await_recv(out_ref.at[:, :, :, :, other_half], so_recv)

    await_recv(xg.at[pl.ds(0, 15 * 48)], sx_send)
    await_recv(hg.at[pl.ds(0, 15 * 144)], sh_send)
    for _ in range(2):
        await_recv(ekt.at[pl.ds(0, 6), pl.ds(0, 224)], se_send)
    await_recv(norms.at[pl.ds(0, 15)], sstat_send.at[3])
    await_recv(across, so_send)
    await_recv(stat_rows.at[pl.ds(0, 15)], sstat_send.at[0])
    await_recv(stat_tm.at[pl.ds(0, 15)], sstat_send.at[1])
    await_recv(stat_two.at[pl.ds(0, 15)], sstat_send.at[2])
    await_recv(sg.at[pl.ds(0, 15 * OWN)], sg_send)

    @pl.when(t < 15)
    def _():
        await_recv(halo_out.at[0], shalo_send.at[0])
        await_recv(halo_out.at[1], shalo_send.at[1])


def shards(
    latents,
    first_gain,
    first_bias,
    second_gain,
    second_bias,
    first_kernel,
    second_kernel,
    expand_kernel,
):
    vmem = pl.BlockSpec(memory_space=pltpu.VMEM)
    anywhere = pl.BlockSpec(memory_space=pl.ANY)
    dma = pltpu.SemaphoreType.DMA
    return pl.pallas_call(
        kernel,
        out_shape=jax.ShapeDtypeStruct((FRAMES, 3, 2, 32, 512), BF16),
        in_specs=[anywhere] + [vmem] * 4 + [anywhere] * 3,
        out_specs=vmem,
        scratch_shapes=[
            pltpu.VMEM((48, CH), BF16),
            pltpu.VMEM((CH, 384), BF16),
            pltpu.VMEM((27 * OWN, CH), BF16),
            pltpu.VMEM((27 * OWN, CH), BF16),
            pltpu.VMEM((FRAMES * PLANE, CH), BF16),
            pltpu.VMEM((FRAMES * PLANE, CH), BF16),
            pltpu.VMEM((FRAMES * CH, PLANE), BF16),
            pltpu.VMEM((FRAMES * CH, PLANE), BF16),
            pltpu.VMEM((12, 256, CH), BF16),
            pltpu.VMEM((TAPS, PLANE), F32),
            pltpu.VMEM((FRAMES, OWN, PLANE), F32),
            pltpu.VMEM((FRAMES, OWN, PLANE), F32),
            pltpu.VMEM((2, 2, OWN, PLANE), F32),
            pltpu.VMEM((2, 2, OWN, PLANE), F32),
            pltpu.VMEM((16, 8, 128), F32),
            pltpu.VMEM((16, 8, 128), F32),
            pltpu.VMEM((16, 8, 128), F32),
            pltpu.VMEM((16, 8, 128), F32),
            pltpu.VMEM((CH, 128), F32),
            pltpu.VMEM((CH, 128), F32),
            pltpu.VMEM((6, FRAMES, 32, 256), BF16),
            pltpu.VMEM((8, OWN, 128), BF16),
            pltpu.VMEM((CH, 128), BF16),
            dma((4,)),
            dma,
            dma((16, FRAMES)),
            dma,
            dma((16, FRAMES)),
            dma,
            dma((2, 8)),
            dma((4,)),
            dma((4,)),
            dma((2,)),
            dma((2,)),
            dma,
            dma,
            dma,
            dma,
        ],
        compiler_params=pltpu.CompilerParams(
            collective_id=0, has_side_effects=True, vmem_limit_bytes=60 << 20
        ),
        name="block",
    )(
        latents.reshape(48, CH),
        first_gain,
        first_bias,
        second_gain,
        second_bias,
        first_kernel.reshape(27 * OWN, CH),
        second_kernel.reshape(27 * OWN, CH),
        expand_kernel,
    ).reshape(3 * FRAMES, 2, 32, 512)


def solution(mesh):
    return jax.shard_map(
        shards,
        mesh=mesh,
        in_specs=(
            P("tm", "rows", None, None),
            P(),
            P(),
            P(),
            P(),
            P(None, None, None, "rows", None),
            P(None, None, None, "rows", None),
            P(None, "rows"),
        ),
        out_specs=P("tm", "rows", None, None),
        check_vma=False,
    )
```

time: 117 us -> 88.6 us (0.76)
  the two profiles are of different devices: /device:TPU:1 before, /device:TPU:2 now
where the time goes in v2:
time: 88.6 us; the launch traced here: 88.5 us
  Pallas kernels  86.6 us (98%)
  local copies, waits for them, and re-layouts  1.93 us (2%)
    pallas_call x1, Pallas kernels, shards(): pl.pallas_call(kernel, out_shape=jax.ShapeDtypeStruct((FRAMES, 3, 2, 32,...  86.6 us
    unnamed x1, local copies, waits for them, and re-layouts  1.93 us

profile of v2, /device:TPU:2, one launch (start us, length us, event | category | flops | bytes accessed | tf_op | source)
XLA Modules:
  0.0 88.5 jit_solution(13691170609552044353)
XLA Ops:
  0.0 86.6 %block.1 = bf16[3,3,2,32,512]{4,3,2,1,0:T(8,128)(2,1)} custom-call(bf16[48,768]{1,0:T(8,128)(2,1)} %bitcast.7, f32[768]{0:T(1024)} %gain1_ref.1, f32[768]{0:T(1024)} %bias1_ref.1, f32[768]{0:T(1024)} %gain2_ref.1, f32[768]{0:T(1024)} %bias2_ref.1, bf16[1296,768]{1,0:T(8,128)(2,1)} %bitcast.5, bf16[1296,768]{1,0:T(8,128)(2,1)} %bitcast.6, bf16[768,384]{1,0:T(8,128)(2,1)} %ek_hbm.1), custom_call_target="tpu_custom_call" | custom-call | tf_op jit(solution)/shard_map/block/pallas_call | solution.py:529
  86.6 1.9 %copy.10 = bf16[9,2,32,512]{3,2,1,0:T(8,128)(2,1)} copy(bf16[9,2,32,512]{3,2,1,0:T(8,128)(2,1)} %bitcast.4) | data formatting | bytes 1179648

commit v3 on v2

--- a/solution.py
+++ b/solution.py
@@ -76,14 +76,18 @@
 
 def kernel(
     x_hbm,
+    gain1_hbm,
+    bias1_hbm,
+    gain2_hbm,
+    bias2_hbm,
+    w1_hbm,
+    w2_hbm,
+    ek_hbm,
+    out_ref,
     gain1_ref,
     bias1_ref,
     gain2_ref,
     bias2_ref,
-    w1_hbm,
-    w2_hbm,
-    ek_hbm,
-    out_ref,
     x_ref,
     ek_ref,
     w1,
@@ -133,33 +137,51 @@
         line = 1 - xh if other else xh
         return line * 8 + lax.rem(z + distance + 8, 8)
 
-    up = (t, slot(False, 1))
-    down = (t, slot(False, -1))
+
     partner = (t, slot(True, 0))
     sibling = (t + 1 - 2 * half, r)
+
+    lines = ((True, 4), (True, 3), (True, -3), (False, 4), (True, 2), (True, -2), (False, 3), (False, -3))
+    lines += ((True, 1), (True, -1), (True, 0), (False, 2), (False, -2), (False, 1), (False, -1))
+    row_peers = [slot(other, distance) for other, distance in lines]
+    block, plane = t // 8, lax.rem(t, 8) // 2
+    steps = ((1, 2), (0, 2), (1, 1), (1, 3), (0, 1), (0, 3), (1, 0))
+    tm_peers = [
+        lax.rem(block + across_x, 2) * 8 + lax.rem(plane + up_y, 4) * 2 + core
+        for across_x, up_y in steps
+        for core in range(2)
+    ] + [t + 1 - 2 * half]
 
     load_x = pltpu.make_async_copy(x_hbm, x_ref, sem_w.at[0])
     load_e = pltpu.make_async_copy(ek_hbm, ek_ref, sem_w.at[1])
     load1 = pltpu.make_async_copy(w1_hbm, w1, sem_w.at[2])
     load2 = pltpu.make_async_copy(w2_hbm, w2, sem_w.at[3])
-    for load in (load_x, load_e, load1, load2):
+    load_small = [
+        pltpu.make_async_copy(src, dst, sem_w.at[4 + i])
+        for i, (src, dst) in enumerate(
+            (
+                (gain1_hbm, gain1_ref),
+                (bias1_hbm, bias1_ref),
+                (gain2_hbm, gain2_ref),
+                (bias2_hbm, bias2_ref),
+            )
+        )
+    ]
+    for load in [load_x, load_e, load1, load2] + load_small:
         load.start()
 
     barrier = pltpu.get_barrier_semaphore()
 
-    def greet(i):
-        pl.semaphore_signal(
-            barrier, inc=1, device_id=(t, lax.rem(r + 1 + i, 16)), device_id_type=MESH
-        )
-        pl.semaphore_signal(
-            barrier, inc=1, device_id=(lax.rem(t + 1 + i, 16), r), device_id_type=MESH
-        )
-
-    loop(15, greet)
+    for peer in row_peers:
+        pl.semaphore_signal(barrier, inc=1, device_id=(t, peer), device_id_type=MESH)
+    for peer in tm_peers:
+        pl.semaphore_signal(barrier, inc=1, device_id=(peer, r), device_id_type=MESH)
 
     load_x.wait()
+    for load in load_small:
+        load.wait()
     for frame in range(FRAMES):
-        xg[pl.ds(pl.multiple_of(frame * PLANE + r * 16, 16), 16)] = x_ref[
+        xg[frame, pl.ds(pl.multiple_of(r * 16, 16), 16)] = x_ref[
             frame * 16 : frame * 16 + 16
         ]
     own = x_ref[...].astype(F32)
@@ -179,16 +201,15 @@
 
     pl.semaphore_wait(barrier, 30)
 
-    def exchange_rows(i):
-        push(
-            stat_rows.at[r],
-            stat_rows.at[r],
-            sstat_send.at[0],
-            sstat.at[0],
-            (t, lax.rem(r + 1 + i, 16)),
-        )
-
-    loop(15, exchange_rows)
+    def tell_rows(ref, place):
+        for peer in row_peers:
+            push(ref, ref, sstat_send.at[place], sstat.at[place], (t, peer))
+
+    def tell_tm(ref, place):
+        for peer in tm_peers:
+            push(ref, ref, sstat_send.at[place], sstat.at[place], (peer, r))
+
+    tell_rows(stat_rows.at[r], 0)
 
     plan = [
         (False, 0, ("x", 2, -2, 1, -1)),
@@ -208,7 +229,7 @@
 
             def piece(i, which=which, devices=devices, place=place):
                 frame = FRAMES - 1 - i
-                ref = view(which, frame)
+                ref = view(which, pl.ds(frame, 1))
                 if place:
                     await_recv(ref, sems.at[which, frame])
                 for device in devices:
@@ -218,26 +239,17 @@
             if place in hooks:
                 hooks[place]()
 
-    def view_x(which, frame):
-        return xg.at[pl.ds(pl.multiple_of(frame * PLANE + which * 16, 16), 16)]
-
-    def view_h(which, frame):
-        return hg.at[pl.ds(pl.multiple_of(frame * CH + which * OWN, 16), OWN)]
+    def view_x(which, frames):
+        return xg.at[frames, pl.ds(pl.multiple_of(which * 16, 16), 16)]
+
+    def view_h(which, frames):
+        return hg.at[frames, pl.ds(pl.multiple_of(which * OWN, 16), OWN)]
 
     def exchange_tm():
         await_recv(stat_rows.at[pl.ds(0, 15)], sstat.at[0])
         stat_tm[t] = jnp.sum(stat_rows[...], axis=0)
 
-        def send(i):
-            push(
-                stat_tm.at[t],
-                stat_tm.at[t],
-                sstat_send.at[1],
-                sstat.at[1],
-                (lax.rem(t + 1 + i, 16), r),
-            )
-
-        loop(15, send)
+        tell_tm(stat_tm.at[t], 1)
 
     def expand_prepare():
         load_e.wait()
@@ -246,7 +258,6 @@
         turned = lax.dot_general(place, ek_ref[...], NT, preferred_element_type=F32).astype(BF16)
         for sub in range(12):
             ekt[sub, pl.ds(pl.multiple_of(z * 32, 32), 32)] = turned[sub * 32 : sub * 32 + 32]
-        expand_start()
 
     def view_e(part, which):
         return ekt.at[pl.ds(part * 6, 6), pl.ds(pl.multiple_of(which * 32, 32), 32)]
@@ -255,6 +266,8 @@
         ref = view_e(half, which)
         push(ref, ref, se_send, se.at[half, which], device)
 
+    up = (t, slot(False, 1))
+    down = (t, slot(False, -1))
     def expand_start():
         send_e(z, up)
         send_e(z, down)
@@ -273,9 +286,8 @@
         which = lax.rem(z + 1 + i, 8)
         await_recv(view_e(1 - half, which), se.at[1 - half, which])
 
-    ring(view_x, sx_send, sx, {0: expand_prepare, 7: exchange_tm})
+    ring(view_x, sx_send, sx, {0: expand_prepare, 5: exchange_tm, 7: expand_start})
     expand_step(1)
-
     await_recv(stat_tm.at[pl.ds(0, 15)], sstat.at[1])
     averages = jnp.sum(stat_tm[...], axis=0) * (1.0 / COUNT)
     mean, square = averages[0:1], averages[1:2]
@@ -291,7 +303,8 @@
 
     def activate(i):
         at = pl.ds(pl.multiple_of(i * 32, 32), 32)
-        act[at] = silu((xg[at].astype(F32) - mean) * scale + bias).astype(BF16)
+        part = pl.ds(pl.multiple_of(lax.rem(i, 8) * 32, 32), 32)
+        act[at] = silu((xg[i // 8, part].astype(F32) - mean) * scale + bias).astype(BF16)
 
     loop(FRAMES * PLANE // 32, activate)
 
@@ -356,7 +369,7 @@
         value.astype(BF16) for value in convolve(w1, product_one, 0, lambda: None)
     ]
     for frame in range(FRAMES):
-        hg[pl.ds(pl.multiple_of(frame * CH + r * OWN, 16), OWN)] = hidden[frame]
+        hg[frame, pl.ds(pl.multiple_of(r * OWN, 16), OWN)] = hidden[frame]
     hidden = [value.astype(F32) for value in hidden]
 
     added = hidden[0] + hidden[1] + hidden[2]
@@ -371,21 +384,12 @@
         message = jnp.where(row8 == i, line, message)
     stat_two[t] = message
 
-    def exchange_two(i):
-        push(
-            stat_two.at[t],
-            stat_two.at[t],
-            sstat_send.at[2],
-            sstat.at[2],
-            (lax.rem(t + 1 + i, 16), r),
-        )
-
     def residuals():
-        loop(15, exchange_two)
+        tell_tm(stat_two.at[t], 2)
         pick = (iota((OWN, CH), 1) == r * OWN + iota((OWN, CH), 0)).astype(BF16)
         for frame in range(FRAMES):
             hid[frame] = lax.dot_general(
-                pick, xg[frame * PLANE : (frame + 1) * PLANE], NT, preferred_element_type=F32
+                pick, xg[frame], NT, preferred_element_type=F32
             )
         gain_columns[...] = jnp.broadcast_to(gain2_ref[...].reshape(1, CH), (128, CH)).T
         bias_columns[...] = jnp.broadcast_to(bias2_ref[...].reshape(1, CH), (128, CH)).T
@@ -402,16 +406,7 @@
             jnp.where(row8 == 1, mean[1:2], jnp.where(row8 == 2, inverse[0:1], inverse[1:2])),
         )
 
-        def send(i):
-            push(
-                norms.at[r],
-                norms.at[r],
-                sstat_send.at[3],
-                sstat.at[3],
-                (t, lax.rem(r + 1 + i, 16)),
-            )
-
-        loop(15, send)
+        tell_rows(norms.at[r], 3)
 
     def after_line():
         spread_two()
@@ -429,7 +424,7 @@
         mean = jnp.where(lower, norm[0:1], norm[1:2])
         scale = jnp.where(lower, norm[2:3], norm[3:4]) * gain_columns[channels]
         bias = bias_columns[channels]
-        value = hg[at].astype(F32)
+        value = hg[i // 16, channels].astype(F32)
         act_two[at] = jnp.concatenate(
             [
                 silu((value[:, part * 128 : part * 128 + 128] - mean) * scale + bias)
@@ -458,46 +453,57 @@
     mine = pl.ds(pl.multiple_of(r * OWN, 16), OWN)
     sg[mine] = pack[z]
 
-    def to_rows(i):
-        other = lax.rem(r + 1 + i, 16)
-        push(pack.at[lax.rem(other, 8)], sg.at[mine], sg_send, sg_recv, (t, other))
-
-    loop(15, to_rows)
+    for peer in row_peers:
+        push(pack.at[lax.rem(peer, 8)], sg.at[mine], sg_send, sg_recv, (t, peer))
     expand_step(4)
     loop(7, expand_last)
-    column = iota((128, PLANE), 1)
-    second = (column >= 96).astype(jnp.int32)
-    inside = column - 96 * second
-    source = 48 * (second + xh - 2 * xh * second) + ((inside >> 5) << 4) + ((inside & 31) >> 1)
-    double = ((iota((128, PLANE), 0) == source) & (column < 192)).astype(BF16)
-    even = (iota((PLANE, PLANE), 1) & 1) == 0
-    await_recv(sg.at[pl.ds(0, 15 * OWN)], sg_recv)
-
-    doubled = jnp.dot(sg[...], double, preferred_element_type=F32).astype(BF16)
+    column = iota((128, 128), 1)
+    inside = ((column >> 5) << 4) + ((column & 31) >> 1)
+
+    def double(line):
+        return ((iota((128, 128), 0) == 48 * line + inside) & (column < 96)).astype(BF16)
+
+    doubles = [double(1 - xh), double(xh)]
+    even = (iota((256, 128), 1) & 1) == 0
     own_half = pl.ds(pl.multiple_of(xh * 256, 256), 256)
     other_half = pl.ds(pl.multiple_of(256 - xh * 256, 256), 256)
-
-    def expand(i):
-        one = jnp.dot(ekt[2 * i], doubled, preferred_element_type=F32)
-        two = jnp.dot(ekt[2 * i + 1], doubled, preferred_element_type=F32)
-        turned = jnp.where(even, one, two).T.astype(BF16)
-        tap_time, tap_row = i // 2, lax.rem(i, 2)
+    await_recv(sg.at[pl.ds(0, 15 * OWN)], sg_recv)
+
+    spread = [
+        jnp.dot(sg[...], matrix, preferred_element_type=F32).astype(BF16) for matrix in doubles
+    ]
+
+    def rows_of(i, positions):
+        both = jnp.dot(
+            ekt[pl.ds(2 * i, 2)].reshape(512, CH), positions, preferred_element_type=F32
+        )
+        return jnp.where(even, both[:256], both[256:]).T.astype(BF16)
+
+    def expand_other(i):
+        turned = rows_of(i, spread[0])
         for frame in range(FRAMES):
-            out_ref[frame, tap_time, tap_row, :, own_half] = turned[frame * 32 : frame * 32 + 32]
-            across[i, frame] = turned[96 + frame * 32 : 128 + frame * 32]
+            across[i, frame] = turned[frame * 32 : frame * 32 + 32]
         push(
             across.at[i],
-            out_ref.at[:, tap_time, tap_row, :, own_half],
+            out_ref.at[:, i // 2, lax.rem(i, 2), :, own_half],
             so_send,
             so_recv,
             partner,
         )
 
-    loop(6, expand)
+    def expand_own(i):
+        turned = rows_of(i, spread[1])
+        for frame in range(FRAMES):
+            out_ref[frame, i // 2, lax.rem(i, 2), :, own_half] = turned[
+                frame * 32 : frame * 32 + 32
+            ]
+
+    loop(6, expand_other)
+    loop(6, expand_own)
     await_recv(out_ref.at[:, :, :, :, other_half], so_recv)
 
-    await_recv(xg.at[pl.ds(0, 15 * 48)], sx_send)
-    await_recv(hg.at[pl.ds(0, 15 * 144)], sh_send)
+    await_recv(xg.at[:, pl.ds(0, 15 * 16)], sx_send)
+    await_recv(hg.at[:, pl.ds(0, 15 * OWN)], sh_send)
     for _ in range(2):
         await_recv(ekt.at[pl.ds(0, 6), pl.ds(0, 224)], se_send)
     await_recv(norms.at[pl.ds(0, 15)], sstat_send.at[3])
@@ -529,16 +535,17 @@
     return pl.pallas_call(
         kernel,
         out_shape=jax.ShapeDtypeStruct((FRAMES, 3, 2, 32, 512), BF16),
-        in_specs=[anywhere] + [vmem] * 4 + [anywhere] * 3,
+        in_specs=[anywhere] * 8,
         out_specs=vmem,
-        scratch_shapes=[
+        scratch_shapes=[pltpu.VMEM((CH,), F32)] * 4
+        + [
             pltpu.VMEM((48, CH), BF16),
             pltpu.VMEM((CH, 384), BF16),
             pltpu.VMEM((27 * OWN, CH), BF16),
             pltpu.VMEM((27 * OWN, CH), BF16),
+            pltpu.VMEM((FRAMES, PLANE, CH), BF16),
             pltpu.VMEM((FRAMES * PLANE, CH), BF16),
-            pltpu.VMEM((FRAMES * PLANE, CH), BF16),
-            pltpu.VMEM((FRAMES * CH, PLANE), BF16),
+            pltpu.VMEM((FRAMES, CH, PLANE), BF16),
             pltpu.VMEM((FRAMES * CH, PLANE), BF16),
             pltpu.VMEM((12, 256, CH), BF16),
             pltpu.VMEM((TAPS, PLANE), F32),
@@ -555,7 +562,7 @@
             pltpu.VMEM((6, FRAMES, 32, 256), BF16),
             pltpu.VMEM((8, OWN, 128), BF16),
             pltpu.VMEM((CH, 128), BF16),
-            dma((4,)),
+            dma((8,)),
             dma,
             dma((16, FRAMES)),
             dma,

time: 88.6 us -> 82.7 us (0.933); the launches traced: 88.5 us -> 81.1 us
  Pallas kernels: 86.6 us -> 79.2 us
    pallas_call x1, Pallas kernels: 86.6 us -> 79.2 us  [shards(): pl.pallas_call(kernel, out_shape=jax.ShapeDtypeStruct((FRAMES, 3, 2, 32,...]
where the time goes in v3:
time: 82.7 us; the launch traced here: 81.1 us
  Pallas kernels  79.2 us (96%)
  local copies, waits for them, and re-layouts  1.93 us (2%)
    pallas_call x1, Pallas kernels, shards(): pl.pallas_call(kernel, out_shape=jax.ShapeDtypeStruct((FRAMES, 3, 2, 32,...  79.2 us
    unnamed x1, local copies, waits for them, and re-layouts  1.93 us

profile of v3, /device:TPU:2, one launch (start us, length us, event | category | flops | bytes accessed | tf_op | source)
XLA Modules:
  0.0 81.1 jit_solution(4972770072605611043)
XLA Ops:
  0.0 79.2 %block.1 = bf16[3,3,2,32,512]{4,3,2,1,0:T(8,128)(2,1)} custom-call(bf16[48,768]{1,0:T(8,128)(2,1)} %bitcast.7, f32[768]{0:T(1024)} %gain1_hbm.1, f32[768]{0:T(1024)} %bias1_hbm.1, f32[768]{0:T(1024)} %gain2_hbm.1, f32[768]{0:T(1024)} %bias2_hbm.1, bf16[1296,768]{1,0:T(8,128)(2,1)} %bitcast.5, bf16[1296,768]{1,0:T(8,128)(2,1)} %bitcast.6, bf16[768,384]{1,0:T(8,128)(2,1)} %ek_hbm.1), custom_call_target="tpu_custom_call" | custom-call | tf_op jit(solution)/shard_map/block/pallas_call | solution.py:535
  79.2 1.9 %copy.10 = bf16[9,2,32,512]{3,2,1,0:T(8,128)(2,1)} copy(bf16[9,2,32,512]{3,2,1,0:T(8,128)(2,1)} %bitcast.4) | data formatting | bytes 1179648

commit v4 on v3

--- a/solution.py
+++ b/solution.py
@@ -94,6 +94,7 @@
     w2,
     xg,
     act,
+    lines_one,
     hg,
     act_two,
     ekt,
@@ -222,7 +223,7 @@
         (False, -4, ("x",)),
     ] + [(True, distance, ()) for distance in (0, -2, 2, -1, 1, -3, 3, -4)]
 
-    def ring(view, send_sem, sems, hooks):
+    def ring(view, send_sem, sems, hooks, ready, arrived):
         for place, (other, distance, targets) in enumerate(plan):
             which = slot(other, distance)
             devices = [partner if to == "x" else (t, slot(False, to)) for to in targets]
@@ -238,6 +239,11 @@
             loop(FRAMES, piece)
             if place in hooks:
                 hooks[place]()
+            if place == 7:
+                ready()
+                loop(8, lambda i: arrived(xh * 8 + i))
+            elif place > 7:
+                arrived(which)
 
     def view_x(which, frames):
         return xg.at[frames, pl.ds(pl.multiple_of(which * 16, 16), 16)]
@@ -286,27 +292,39 @@
         which = lax.rem(z + 1 + i, 8)
         await_recv(view_e(1 - half, which), se.at[1 - half, which])
 
-    ring(view_x, sx_send, sx, {0: expand_prepare, 5: exchange_tm, 7: expand_start})
+    row8 = iota((8, 128), 0)
+
+    def ready_one():
+        await_recv(stat_tm.at[pl.ds(0, 15)], sstat.at[1])
+        averages = jnp.sum(stat_tm[...], axis=0) * (1.0 / COUNT)
+        mean, square = averages[0:1], averages[1:2]
+        inverse = lax.rsqrt(square - mean * mean + 1e-06)
+        spreads = jnp.where(row8 == 0, mean, jnp.where(row8 == 1, inverse, 0.0))
+        per_channel = jnp.dot(
+            spreads, group_matrix((128, CH), 0), precision=HIGH, preferred_element_type=F32
+        )
+        lines_one[0] = jnp.broadcast_to(per_channel[0:1], (8, CH))
+        lines_one[1] = jnp.broadcast_to(per_channel[1:2] * gain1_ref[...].reshape(1, CH), (8, CH))
+        lines_one[2] = jnp.broadcast_to(bias1_ref[...].reshape(1, CH), (8, CH))
+
+    def arrived_one(which):
+        part = pl.ds(pl.multiple_of(which * 16, 16), 16)
+        mean, scale, bias = (lines_one[i, 0:1] for i in range(3))
+
+        def activate(frame):
+            act[frame, part] = silu((xg[frame, part].astype(F32) - mean) * scale + bias).astype(BF16)
+
+        loop(FRAMES, activate)
+
+    ring(
+        view_x,
+        sx_send,
+        sx,
+        {0: expand_prepare, 3: exchange_tm, 7: expand_start},
+        ready_one,
+        arrived_one,
+    )
     expand_step(1)
-    await_recv(stat_tm.at[pl.ds(0, 15)], sstat.at[1])
-    averages = jnp.sum(stat_tm[...], axis=0) * (1.0 / COUNT)
-    mean, square = averages[0:1], averages[1:2]
-    inverse = lax.rsqrt(square - mean * mean + 1e-06)
-    row8 = iota((8, 128), 0)
-    spreads = jnp.where(row8 == 0, mean, jnp.where(row8 == 1, inverse, 0.0))
-    per_channel = jnp.dot(
-        spreads, group_matrix((128, CH), 0), precision=HIGH, preferred_element_type=F32
-    )
-    mean = per_channel[0:1]
-    scale = per_channel[1:2] * gain1_ref[...].reshape(1, CH)
-    bias = bias1_ref[...].reshape(1, CH)
-
-    def activate(i):
-        at = pl.ds(pl.multiple_of(i * 32, 32), 32)
-        part = pl.ds(pl.multiple_of(lax.rem(i, 8) * 32, 32), 32)
-        act[at] = silu((xg[i // 8, part].astype(F32) - mean) * scale + bias).astype(BF16)
-
-    loop(FRAMES * PLANE // 32, activate)
 
     to_next = (lax.rem(t + 1, 16), r)
 
@@ -357,12 +375,10 @@
         ]
 
     def product_one(rows, frame):
-        at = pl.ds(pl.multiple_of(frame * PLANE, PLANE), PLANE)
-        return lax.dot_general(rows, act[at], NT, preferred_element_type=F32)
+        return lax.dot_general(rows, act[frame], NT, preferred_element_type=F32)
 
     def product_two(rows, frame):
-        at = pl.ds(pl.multiple_of(frame * CH, CH), CH)
-        return jnp.dot(rows, act_two[at], preferred_element_type=F32)
+        return jnp.dot(rows, act_two[frame], preferred_element_type=F32)
 
     load1.wait()
     hidden = [
@@ -408,33 +424,40 @@
 
         tell_rows(norms.at[r], 3)
 
-    def after_line():
-        spread_two()
-        expand_step(2)
-
-    ring(view_h, sh_send, sh, {0: residuals, 7: after_line})
-    await_recv(norms.at[pl.ds(0, 15)], sstat.at[3])
     lower = iota((OWN, 128), 0) < 24
 
-    def activate_two(i):
-        source = lax.rem(i, 16)
-        at = pl.ds(pl.multiple_of(i * OWN, 16), OWN)
-        channels = pl.ds(pl.multiple_of(source * OWN, 16), OWN)
-        norm = norms[source]
+    def ready_two():
+        await_recv(norms.at[pl.ds(0, 15)], sstat.at[3])
+
+    def arrived_two(which):
+        channels = pl.ds(pl.multiple_of(which * OWN, 16), OWN)
+        norm = norms[which]
         mean = jnp.where(lower, norm[0:1], norm[1:2])
         scale = jnp.where(lower, norm[2:3], norm[3:4]) * gain_columns[channels]
         bias = bias_columns[channels]
-        value = hg[i // 16, channels].astype(F32)
-        act_two[at] = jnp.concatenate(
-            [
-                silu((value[:, part * 128 : part * 128 + 128] - mean) * scale + bias)
-                for part in range(2)
-            ],
-            axis=1,
-        ).astype(BF16)
+
+        def activate(frame):
+            value = hg[frame, channels].astype(F32)
+            act_two[frame, channels] = jnp.concatenate(
+                [
+                    silu((value[:, part * 128 : part * 128 + 128] - mean) * scale + bias)
+                    for part in range(2)
+                ],
+                axis=1,
+            ).astype(BF16)
+
+        loop(FRAMES, activate)
+
+    ring(
+        view_h,
+        sh_send,
+        sh,
+        {0: residuals, 3: spread_two, 7: lambda: expand_step(2)},
+        ready_two,
+        arrived_two,
+    )
 
     load2.wait()
-    loop(16 * FRAMES, activate_two)
     sums = convolve(w2, product_two, 1, lambda: expand_step(3))
     for frame in range(FRAMES):
         hid[frame] = (sums[frame] + hid[frame]).astype(BF16).astype(F32)
@@ -544,9 +567,10 @@
             pltpu.VMEM((27 * OWN, CH), BF16),
             pltpu.VMEM((27 * OWN, CH), BF16),
             pltpu.VMEM((FRAMES, PLANE, CH), BF16),
-            pltpu.VMEM((FRAMES * PLANE, CH), BF16),
+            pltpu.VMEM((FRAMES, PLANE, CH), BF16),
+            pltpu.VMEM((3, 8, CH), F32),
             pltpu.VMEM((FRAMES, CH, PLANE), BF16),
-            pltpu.VMEM((FRAMES * CH, PLANE), BF16),
+            pltpu.VMEM((FRAMES, CH, PLANE), BF16),
             pltpu.VMEM((12, 256, CH), BF16),
             pltpu.VMEM((TAPS, PLANE), F32),
             pltpu.VMEM((FRAMES, OWN, PLANE), F32),

time: 82.7 us -> 79.4 us (0.960); the launches traced: 81.1 us -> 79.2 us
  Pallas kernels: 79.2 us -> 77.3 us
    pallas_call x1, Pallas kernels: 79.2 us -> 77.3 us  [shards(): pl.pallas_call(kernel, out_shape=jax.ShapeDtypeStruct((FRAMES, 3, 2, 32,...]
where the time goes in v4:
time: 79.4 us; the launch traced here: 79.2 us
  Pallas kernels  77.3 us (97%)
  local copies, waits for them, and re-layouts  1.93 us (2%)
    pallas_call x1, Pallas kernels, shards(): pl.pallas_call(kernel, out_shape=jax.ShapeDtypeStruct((FRAMES, 3, 2, 32,...  77.3 us
    unnamed x1, local copies, waits for them, and re-layouts  1.93 us

profile of v4, /device:TPU:2, one launch (start us, length us, event | category | flops | bytes accessed | tf_op | source)
XLA Modules:
  0.0 79.2 jit_solution(8095767262140947473)
XLA Ops:
  0.0 77.3 %block.1 = bf16[3,3,2,32,512]{4,3,2,1,0:T(8,128)(2,1)} custom-call(bf16[48,768]{1,0:T(8,128)(2,1)} %bitcast.7, f32[768]{0:T(1024)} %gain1_hbm.1, f32[768]{0:T(1024)} %bias1_hbm.1, f32[768]{0:T(1024)} %gain2_hbm.1, f32[768]{0:T(1024)} %bias2_hbm.1, bf16[1296,768]{1,0:T(8,128)(2,1)} %bitcast.5, bf16[1296,768]{1,0:T(8,128)(2,1)} %bitcast.6, bf16[768,384]{1,0:T(8,128)(2,1)} %ek_hbm.1), custom_call_target="tpu_custom_call" | custom-call | tf_op jit(solution)/shard_map/block/pallas_call | solution.py:558
  77.3 1.9 %copy.10 = bf16[9,2,32,512]{3,2,1,0:T(8,128)(2,1)} copy(bf16[9,2,32,512]{3,2,1,0:T(8,128)(2,1)} %bitcast.4) | data formatting | bytes 1179648

commit v5 on v4

--- a/solution.py
+++ b/solution.py
@@ -223,7 +223,13 @@
         (False, -4, ("x",)),
     ] + [(True, distance, ()) for distance in (0, -2, 2, -1, 1, -3, 3, -4)]
 
-    def ring(view, send_sem, sems, hooks, ready, arrived):
+    def start_frame(view, send_sem, sems, frame):
+        ref = view(r, pl.ds(frame, 1))
+        for to in plan[0][2]:
+            device = partner if to == "x" else (t, slot(False, to))
+            push(ref, ref, send_sem, sems.at[r, frame], device)
+
+    def ring(view, send_sem, sems, hooks, ready, arrived, begun=0):
         for place, (other, distance, targets) in enumerate(plan):
             which = slot(other, distance)
             devices = [partner if to == "x" else (t, slot(False, to)) for to in targets]
@@ -236,7 +242,10 @@
                 for device in devices:
                     push(ref, ref, send_sem, sems.at[which, frame], device)
 
-            loop(FRAMES, piece)
+            if place == 0 and begun:
+                loop(FRAMES - begun, lambda i, piece=piece: piece(i + begun))
+            else:
+                loop(FRAMES, piece)
             if place in hooks:
                 hooks[place]()
             if place == 7:
@@ -328,7 +337,7 @@
 
     to_next = (lax.rem(t + 1, 16), r)
 
-    def convolve(weights, product, which, between):
+    def convolve(weights, product, which, between, early):
         def result(i):
             out_frame = 4 - i
             first = jnp.maximum(out_frame - 2, 0)
@@ -363,6 +372,7 @@
         loop(2, ahead)
         between()
         loop(3, own)
+        early()
 
         @pl.when(t > 0)
         def _():
@@ -380,11 +390,15 @@
     def product_two(rows, frame):
         return jnp.dot(rows, act_two[frame], preferred_element_type=F32)
 
+    def first_frame():
+        hg[2, pl.ds(pl.multiple_of(r * OWN, 16), OWN)] = results[2].astype(BF16)
+        start_frame(view_h, sh_send, sh, 2)
+
     load1.wait()
     hidden = [
-        value.astype(BF16) for value in convolve(w1, product_one, 0, lambda: None)
+        value.astype(BF16) for value in convolve(w1, product_one, 0, lambda: None, first_frame)
     ]
-    for frame in range(FRAMES):
+    for frame in range(FRAMES - 1):
         hg[frame, pl.ds(pl.multiple_of(r * OWN, 16), OWN)] = hidden[frame]
     hidden = [value.astype(F32) for value in hidden]
 
@@ -455,10 +469,11 @@
         {0: residuals, 3: spread_two, 7: lambda: expand_step(2)},
         ready_two,
         arrived_two,
+        1,
     )
 
     load2.wait()
-    sums = convolve(w2, product_two, 1, lambda: expand_step(3))
+    sums = convolve(w2, product_two, 1, lambda: expand_step(3), lambda: None)
     for frame in range(FRAMES):
         hid[frame] = (sums[frame] + hid[frame]).astype(BF16).astype(F32)
 
@@ -557,7 +572,7 @@
     dma = pltpu.SemaphoreType.DMA
     return pl.pallas_call(
         kernel,
-        out_shape=jax.ShapeDtypeStruct((FRAMES, 3, 2, 32, 512), BF16),
+        out_shape=pltpu.VMEM((FRAMES, 3, 2, 32, 512), BF16),
         in_specs=[anywhere] * 8,
         out_specs=vmem,
         scratch_shapes=[pltpu.VMEM((CH,), F32)] * 4
@@ -603,18 +618,23 @@
             dma,
         ],
         compiler_params=pltpu.CompilerParams(
-            collective_id=0, has_side_effects=True, vmem_limit_bytes=60 << 20
+            collective_id=0, has_side_effects=True, vmem_limit_bytes=48 << 20
         ),
         name="block",
     )(
-        latents.reshape(48, CH),
-        first_gain,
-        first_bias,
-        second_gain,
-        second_bias,
-        first_kernel.reshape(27 * OWN, CH),
-        second_kernel.reshape(27 * OWN, CH),
-        expand_kernel,
+        *[
+            pltpu.with_memory_space_constraint(array, pltpu.HBM)
+            for array in (
+                latents.reshape(48, CH),
+                first_gain,
+                first_bias,
+                second_gain,
+                second_bias,
+                first_kernel.reshape(27 * OWN, CH),
+                second_kernel.reshape(27 * OWN, CH),
+                expand_kernel,
+            )
+        ]
     ).reshape(3 * FRAMES, 2, 32, 512)
 
 

time: 79.4 us -> 77.4 us (0.975)
  local copies, waits for them, and re-layouts: 1.93 us -> 0.82 us
  Pallas kernels: 77.3 us -> 76.4 us
    unnamed x1, local copies, waits for them, and re-layouts: 1.93 us -> 0.82 us
    pallas_call x1, Pallas kernels: 77.3 us -> 76.4 us  [shards(): pl.pallas_call(kernel, out_shape=pltpu.VMEM((FRAMES, 3, 2, 32, 512), BF16...]
where the time goes in v5:
time: 77.4 us; the launch traced here: 77.2 us
  Pallas kernels  76.4 us (99%)
  local copies, waits for them, and re-layouts  0.82 us (1%)
    pallas_call x1, Pallas kernels, shards(): pl.pallas_call(kernel, out_shape=pltpu.VMEM((FRAMES, 3, 2, 32, 512), BF16...  76.4 us

profile of v5, /device:TPU:2, one launch (start us, length us, event | category | flops | bytes accessed | tf_op | source)
XLA Modules:
  0.0 77.2 jit_solution(17641907879059039559)
XLA Ops:
  0.0 76.4 %block.1 = bf16[3,3,2,32,512]{4,3,2,1,0:T(8,128)(2,1)S(1)} custom-call(bf16[48,768]{1,0:T(8,128)(2,1)} %bitcast.7, f32[768]{0:T(1024)} %gain1_hbm.1, f32[768]{0:T(1024)} %bias1_hbm.1, f32[768]{0:T(1024)} %gain2_hbm.1, f32[768]{0:T(1024)} %bias2_hbm.1, bf16[1296,768]{1,0:T(8,128)(2,1)} %bitcast.5, bf16[1296,768]{1,0:T(8,128)(2,1)} %bitcast.6, ...), custom_call_target="tpu_custom_call" | custom-call | tf_op jit(solution)/shard_map/block/pallas_call | solution.py:573
  76.4 0.8 %copy.10 = bf16[9,2,32,512]{3,2,1,0:T(8,128)(2,1)} copy(bf16[9,2,32,512]{3,2,1,0:T(8,128)(2,1)S(1)} %bitcast.4) | data formatting | bytes 1179648

commit v6 on v5

--- a/solution.py
+++ b/solution.py
@@ -153,6 +153,13 @@
         for core in range(2)
     ] + [t + 1 - 2 * half]
 
+    barrier = pltpu.get_barrier_semaphore()
+
+    for peer in row_peers:
+        pl.semaphore_signal(barrier, inc=1, device_id=(t, peer), device_id_type=MESH)
+    for peer in tm_peers:
+        pl.semaphore_signal(barrier, inc=1, device_id=(peer, r), device_id_type=MESH)
+
     load_x = pltpu.make_async_copy(x_hbm, x_ref, sem_w.at[0])
     load_e = pltpu.make_async_copy(ek_hbm, ek_ref, sem_w.at[1])
     load1 = pltpu.make_async_copy(w1_hbm, w1, sem_w.at[2])
@@ -168,19 +175,10 @@
             )
         )
     ]
-    for load in [load_x, load_e, load1, load2] + load_small:
+    for load in [load_x] + load_small + [load_e, load1, load2]:
         load.start()
 
-    barrier = pltpu.get_barrier_semaphore()
-
-    for peer in row_peers:
-        pl.semaphore_signal(barrier, inc=1, device_id=(t, peer), device_id_type=MESH)
-    for peer in tm_peers:
-        pl.semaphore_signal(barrier, inc=1, device_id=(peer, r), device_id_type=MESH)
-
     load_x.wait()
-    for load in load_small:
-        load.wait()
     for frame in range(FRAMES):
         xg[frame, pl.ds(pl.multiple_of(r * 16, 16), 16)] = x_ref[
             frame * 16 : frame * 16 + 16
@@ -200,6 +198,8 @@
     def _():
         halo_in[...] = jnp.zeros_like(halo_in)
 
+    for load in load_small:
+        load.wait()
     pl.semaphore_wait(barrier, 30)
 
     def tell_rows(ref, place):

time: 77.4 us -> 77.4 us (level)
  no operation moved by 1% of the time
where the time goes in v6:
time: 77.4 us; the launch traced here: 77.1 us
  Pallas kernels  76.3 us (99%)
  local copies, waits for them, and re-layouts  0.82 us (1%)
    pallas_call x1, Pallas kernels, shards(): pl.pallas_call(kernel, out_shape=pltpu.VMEM((FRAMES, 3, 2, 32, 512), BF16...  76.3 us

profile of v6, /device:TPU:2, one launch (start us, length us, event | category | flops | bytes accessed | tf_op | source)
XLA Modules:
  0.0 77.1 jit_solution(699780256830202692)
XLA Ops:
  0.0 76.3 %block.1 = bf16[3,3,2,32,512]{4,3,2,1,0:T(8,128)(2,1)S(1)} custom-call(bf16[48,768]{1,0:T(8,128)(2,1)} %bitcast.7, f32[768]{0:T(1024)} %gain1_hbm.1, f32[768]{0:T(1024)} %bias1_hbm.1, f32[768]{0:T(1024)} %gain2_hbm.1, f32[768]{0:T(1024)} %bias2_hbm.1, bf16[1296,768]{1,0:T(8,128)(2,1)} %bitcast.5, bf16[1296,768]{1,0:T(8,128)(2,1)} %bitcast.6, ...), custom_call_target="tpu_custom_call" | custom-call | tf_op jit(solution)/shard_map/block/pallas_call | solution.py:573
  76.3 0.8 %copy.10 = bf16[9,2,32,512]{3,2,1,0:T(8,128)(2,1)} copy(bf16[9,2,32,512]{3,2,1,0:T(8,128)(2,1)S(1)} %bitcast.4) | data formatting | bytes 1179648
